TPU v7x, 32 devices: a whole 2x2x4 slice. The times are simulated.
32 devices in a mesh: sec: 4 (over x, core), op: 8 (over z, y).
Axes of the slice: x: 2, y: 2, z: 4, core: 2. Of those that a mesh axis runs over, the one named last changes fastest.
Arguments:
- wavefunction: bfloat16 [4, 768, 768], P('sec', 'op'), may hold values from -6 to 6
- left_ops: bfloat16 [4, 24, 768, 768], P('sec', 'op'), may hold values from -0.046875 to 0.046875
- right_ops: bfloat16 [4, 24, 768, 768], P('sec', 'op'), may hold values from -0.21875 to 0.21875
- diagonal: float32 [4, 768, 768], P('sec', 'op'), may hold values from 0.15 to 10.2
- sector_sizes: int32 [4], P('sec'), may hold values from 192 to 768
- partner: int32 [4], replicated, may hold values from 0 to 3, as said below
Outputs:
- updated: float32 [4, 768, 768], P('sec', 'op')
- residual: float32 [4, 768, 768], P('sec', 'op')
Inputs may be any that keep to these rules, and one draw needn't show every extreme that they name: `partner`: each sector is named exactly once.
All inputs are finite; a program needn't handle non-finite values.
Results may differ from a plain program's by a relative error of at most 0.0017.
Values may be sent and summed in bfloat16 or wider, within the bound.
A program may use at most 64 MiB of HBM per device.

v0:
```python
import functools

import jax
import jax.numpy as jnp
from jax import lax
from jax.experimental import pallas as pl
from jax.experimental.pallas import tpu as pltpu
from jax.sharding import PartitionSpec as P

MESH = pl.DeviceIdType.MESH
F32 = jnp.float32
BF16 = jnp.bfloat16
PAIR = 2


def nt_dot(a, b):
    return lax.dot_general(a, b, (((1,), (1,)), ((), ())), preferred_element_type=F32)


def nn_dot(a, b):
    return lax.dot_general(a, b, (((1,), (0,)), ((), ())), preferred_element_type=F32)


def fold_sum(value):
    rows, width = value.shape
    part = jnp.sum(value.reshape(rows // 8, 8, width), axis=0)
    total = part[:, :128]
    for start in range(128, width, 128):
        total = total + part[:, start : start + 128]
    return total


def kernel(
    sectors, ops,
    partner_ref, sizes_ref, wave_ref, diag_ref, left_hbm, right_hbm,
    sigma_ref, energy_ref,
    left, right, left_t, blocks, own_full, other_full, acc,
    adj_keep, adj_ys, adj_yr, adj_zs, adj_zr, routed,
    dir_keep, dir_ys, dir_yr, dir_zs, dir_zr,
    scalars, scalar_y, scalar_z, scalar_s,
    load_sem,
    chain_send, chain_recv, near_send, near_recv,
    sec_send, sec_recv, mate_send, mate_recv, route_send, route_recv,
    adj_send, adj_recv, dir_send, dir_recv, sc_send, sc_recv,
):
    far_count = ops // PAIR
    sec_far = sectors // PAIR
    me_sec = lax.axis_index("sec")
    me_op = lax.axis_index("op")
    far, near = me_op // PAIR, lax.rem(me_op, PAIR)
    chip, core = me_sec // PAIR, lax.rem(me_sec, PAIR)
    rows, width = wave_ref.shape[1:]
    terms = left.shape[0]

    def far_at(step):
        return lax.rem(far + step + far_count, far_count)

    def sec_at(step):
        return lax.rem(me_sec + step + sectors, sectors)

    def chip_at(step):
        return lax.rem(chip + step + sec_far, sec_far) * PAIR

    near_peer = (me_sec, far * PAIR + (1 - near))
    up_peer = (me_sec, me_op + PAIR)
    down_peer = (me_sec, me_op - PAIR)
    mate = (chip * PAIR + (1 - core), me_op)

    def far_peer(step):
        return (me_sec, far_at(step) * PAIR + near)

    def sec_peer(step):
        return (sec_at(step), me_op)

    def chip_peer(step):
        return (chip_at(step) + core, me_op)

    def remote(src, dst, send, recv, device):
        return pltpu.make_async_remote_copy(
            src_ref=src, dst_ref=dst, send_sem=send, recv_sem=recv, device_id=device, device_id_type=MESH
        )

    started = []

    def send(*args):
        remote(*args).start()
        started.append((None, args))

    def send_if(cond, *args):
        @pl.when(cond)
        def _():
            remote(*args).start()

        started.append((cond, args))

    def recv(dst, send_sem, recv_sem):
        remote(dst, dst, send_sem, recv_sem, near_peer).wait_recv()

    load_left = pltpu.make_async_copy(left_hbm.at[0], left, load_sem.at[0])
    load_right = pltpu.make_async_copy(right_hbm.at[0], right, load_sem.at[1])
    load_left.start()
    load_right.start()

    barrier = pltpu.get_barrier_semaphore()
    peers = [near_peer]
    peers += [far_peer(step) for step in range(1, far_count)]
    peers += [sec_peer(step) for step in range(1, sectors)]
    for peer in peers:
        pl.semaphore_signal(barrier, inc=1, device_id=peer, device_id_type=MESH)

    size = sizes_ref[0]
    row_index = me_op * rows + lax.broadcasted_iota(jnp.int32, (rows, width), 0)
    col_index = lax.broadcasted_iota(jnp.int32, (rows, width), 1)
    live_mask = (row_index < size) & (col_index < size)
    wave = jnp.where(live_mask, wave_ref[0].astype(F32), 0.0)
    blocks[me_sec, near, far] = wave.astype(BF16)
    diag = diag_ref[0]
    scalars[0] = fold_sum(diag * wave * wave)
    scalars[1] = fold_sum(wave * wave)
    pl.semaphore_wait(barrier, len(peers))

    has_up, has_down = far + 1 < far_count, far > 0

    def to_chips(cond, half, place):
        block = blocks.at[me_sec, half, place]
        for step in range(1, sec_far):
            args = (block, block, sec_send.at[step, half, place], sec_recv.at[step, half], chip_peer(step))
            send(*args) if cond is None else send_if(cond, *args)

    mine = blocks.at[me_sec, near, far]
    send_if(has_up, mine, mine, chain_send.at[0, far], chain_recv.at[far], up_peer)
    send_if(has_down, mine, mine, chain_send.at[1, far], chain_recv.at[far], down_peer)
    send(mine, mine, near_send.at[far], near_recv.at[far], near_peer)
    to_chips(None, near, far)

    def arrive(cond, place, onward, way, peer):
        block = blocks.at[me_sec, near, place]

        @pl.when(cond)
        def _():
            recv(block, chain_send.at[way, place], chain_recv.at[place])

        send_if(cond & onward, block, block, chain_send.at[way, place], chain_recv.at[place], peer)
        send_if(cond, block, block, near_send.at[place], near_recv.at[place], near_peer)
        to_chips(cond, near, place)

    load_left.wait()

    def turn(term, carry):
        left_t[term] = left[term].T
        return carry

    turned = 0
    for step in range(1, far_count):
        if turned < terms:
            turn(turned, 0)
            turned += 1
        arrive(far - step >= 0, jnp.maximum(far - step, 0), has_up, 0, up_peer)
        arrive(far + step < far_count, jnp.minimum(far + step, far_count - 1), has_down, 1, down_peer)
    for term in range(turned, terms):
        turn(term, 0)

    def to_mate(sector, step, half):
        part = blocks.at[sector, half]
        send(part, part, mate_send.at[step, half], mate_recv.at[step, half], mate)

    to_mate(me_sec, 0, near)
    for step in range(far_count):
        place = far_at(-step)
        recv(blocks.at[me_sec, 1 - near, place], near_send.at[place], near_recv.at[place])
        to_chips(None, 1 - near, place)
    to_mate(me_sec, 0, 1 - near)

    def assemble(sector, full):
        for place in range(far_count):
            pair = [blocks[sector, half, place] for half in range(PAIR)]
            if rows % 16:
                pair = [part.astype(F32) for part in pair]
            full[place * span : (place + 1) * span, :] = jnp.concatenate(pair, axis=0).astype(BF16)

    span = PAIR * rows
    assemble(me_sec, own_full)
    load_right.wait()

    order = list(range(1, far_count)) + [0]
    half = (far_count + 1) // 2
    groups = [order[:half], order[half:]]

    def place_of(step):
        return pl.ds(pl.multiple_of(far_at(step) * span, span), span)

    def products(group, base, left_side, middle, last_dot, keep, ys, yr, sends, recvs):
        total = acc.at[pl.ds(base, len(group) * span)]

        def one(term, carry):
            lhs = jnp.concatenate([left_side[term, place_of(step), :] for step in group], axis=0)
            inner = nn_dot(lhs, middle[...]).astype(BF16)
            out = last_dot(inner, right[term])

            @pl.when(term == 0)
            def _():
                total[...] = out

            @pl.when(term > 0)
            def _():
                total[...] += out

            return carry

        lax.fori_loop(0, terms, one, 0)
        for at, step in enumerate(group):
            start = base + at * span
            first = acc[start : start + rows, :]
            second = acc[start + rows : start + span, :]
            keep[step] = jnp.where(near == 0, first, second)
            ys[step] = jnp.where(near == 0, second, first).astype(BF16)
            send(ys.at[step], yr.at[step], sends.at[step], recvs.at[step], near_peer)

    def inner_product(group, base, weight):
        for at, step in enumerate(group):
            start = base + at * span
            scalars[0] += fold_sum(acc[start : start + span, :] * weight[place_of(step), :].astype(F32))

    def pass_on(step, keep, yr, zs, zr, sends, recvs):
        recv(yr.at[step], sends.at[step], recvs.at[step])
        summed = keep[step] + yr[step].astype(F32)
        if step == 0:
            keep[0] = summed
        else:
            zs[step] = summed.astype(BF16)
            at = far_count + step
            send(zs.at[step], zr.at[step], sends.at[at], recvs.at[at], far_peer(step))

    def finish(keep, zr, sends, recvs):
        total = keep[0]
        for step in range(1, far_count):
            at = far_count + step
            recv(zr.at[step], sends.at[at], recvs.at[at])
            total = total + zr[step].astype(F32)
        return total

    def from_chips(half):
        for step in range(1, sec_far):
            sector = chip_at(-step) + core
            recv(blocks.at[sector, half], sec_send.at[step, half, 0], sec_recv.at[step, half])
            to_mate(sector, step, half)

    adj = (adj_keep, adj_ys, adj_yr, adj_send, adj_recv)
    direct = (dir_keep, dir_ys, dir_yr, dir_send, dir_recv)
    adj_pass = (adj_keep, adj_yr, adj_zs, adj_zr, adj_send, adj_recv)
    dir_pass = (dir_keep, dir_yr, dir_zs, dir_zr, dir_send, dir_recv)
    second_base = len(groups[0]) * span

    products(groups[0], 0, left_t, own_full, nn_dot, *adj)
    from_chips(near)
    products(groups[1], second_base, left_t, own_full, nn_dot, *adj)
    for step in groups[0]:
        pass_on(step, *adj_pass)
    from_chips(1 - near)
    for step in range(sec_far):
        sector = chip_at(-step) + (1 - core)
        for side in (near, 1 - near):
            recv(blocks.at[sector, side], mate_send.at[step, side], mate_recv.at[step, side])
    assemble(partner_ref[me_sec], other_full)
    inner_product(groups[0], 0, other_full)
    inner_product(groups[1], second_base, other_full)

    products(groups[0], 0, left, other_full, nt_dot, *direct)
    for step in groups[1]:
        pass_on(step, *adj_pass)
    products(groups[1], second_base, left, other_full, nt_dot, *direct)
    for step in groups[0]:
        pass_on(step, *dir_pass)
    inner_product(groups[0], 0, own_full)
    inner_product(groups[1], second_base, own_full)

    send(scalars, scalar_y, sc_send.at[0], sc_recv.at[0], near_peer)
    routed[me_sec] = finish(adj_keep, adj_zr, adj_send, adj_recv)
    rows_out = routed.at[me_sec]
    for step in range(1, sec_far):
        send(rows_out, rows_out, route_send.at[0, step], route_recv.at[0, step], chip_peer(step))
    send(rows_out, rows_out, route_send.at[1, 0], route_recv.at[1, 0], mate)
    recv(scalar_y, sc_send.at[0], sc_recv.at[0])
    scalar_z[0] = scalars[...] + scalar_y[...]
    for step in range(1, far_count):
        send(scalar_z.at[0], scalar_z.at[step], sc_send.at[step], sc_recv.at[step], far_peer(step))
    for step in groups[1]:
        pass_on(step, *dir_pass)

    inner_sum = scalar_z[0]
    for step in range(1, far_count):
        recv(scalar_z.at[step], sc_send.at[step], sc_recv.at[step])
        inner_sum = inner_sum + scalar_z[step]
    scalar_s[0] = inner_sum
    for step in range(1, sectors):
        at = far_count + step
        send(scalar_s.at[0], scalar_s.at[step], sc_send.at[at], sc_recv.at[at], sec_peer(step))
    for step in range(1, sec_far):
        part = routed.at[chip_at(-step) + core]
        recv(part, route_send.at[0, step], route_recv.at[0, step])
        send(part, part, route_send.at[1, step], route_recv.at[1, step], mate)
    for step in range(1, sectors):
        at = far_count + step
        recv(scalar_s.at[step], sc_send.at[at], sc_recv.at[at])
        inner_sum = inner_sum + scalar_s[step]
    energy_ref[...] = jnp.sum(inner_sum[0], keepdims=True) / jnp.sum(inner_sum[1], keepdims=True)

    source = jnp.int32(0)
    for sector in range(sectors):
        source = jnp.where(partner_ref[sector] == me_sec, sector, source)
    for step in range(sec_far):
        recv(routed.at[chip_at(-step) + (1 - core)], route_send.at[1, step], route_recv.at[1, step])
    other_part = routed[source] + diag_ref[0] * wave
    direct_part = finish(dir_keep, dir_zr, dir_send, dir_recv)
    sigma_ref[0] = jnp.where(live_mask, direct_part + other_part, 0.0)

    for cond, args in started:
        if cond is None:
            remote(*args).wait_send()
        else:

            @pl.when(cond)
            def _():
                remote(*args).wait_send()


def per_device(sectors, ops, wavefunction, left_ops, right_ops, diagonal, sector_sizes, partner):
    _, rows, width = wavefunction.shape
    terms, height = left_ops.shape[1:3]
    far_count = ops // PAIR
    block16 = pltpu.VMEM((far_count, rows, width), BF16)
    block32 = pltpu.VMEM((far_count, rows, width), F32)
    sec_far = sectors // PAIR
    full = pltpu.VMEM((height, width), BF16)
    operators = pltpu.VMEM((terms, height, width), BF16)
    dma = pltpu.SemaphoreType.DMA
    vmem = pl.BlockSpec(memory_space=pltpu.VMEM)
    smem = pl.BlockSpec(memory_space=pltpu.SMEM)
    hbm = pl.BlockSpec(memory_space=pl.ANY)
    sigma, energy = pl.pallas_call(
        functools.partial(kernel, sectors, ops),
        out_shape=(
            jax.ShapeDtypeStruct((1, rows, width), F32),
            jax.ShapeDtypeStruct((1, 1), F32),
        ),
        in_specs=[smem, smem, vmem, vmem, hbm, hbm],
        out_specs=(vmem, vmem),
        scratch_shapes=[
            operators, operators, operators,
            pltpu.VMEM((sectors, PAIR, far_count, rows, width), BF16),
            full, full,
            pltpu.VMEM((height, width), F32),
            block32, block16, block16, block16, block16,
            pltpu.VMEM((sectors, rows, width), F32),
            block32, block16, block16, block16, block16,
            pltpu.VMEM((2, 8, 128), F32),
            pltpu.VMEM((2, 8, 128), F32),
            pltpu.VMEM((far_count, 2, 8, 128), F32),
            pltpu.VMEM((sectors, 2, 8, 128), F32),
            dma((2,)),
            dma((2, far_count)), *[dma((far_count,))] * 3,
            dma((sec_far, PAIR, far_count)), dma((sec_far, PAIR)),
            *[dma((sec_far, PAIR))] * 2,
            *[dma((2, sec_far))] * 2,
            *[dma((2 * far_count,))] * 4,
            *[dma((far_count + sectors,))] * 2,
        ],
        compiler_params=pltpu.CompilerParams(
            collective_id=0, has_side_effects=True, vmem_limit_bytes=56 * 1024 * 1024
        ),
        cost_estimate=pl.CostEstimate(
            flops=8 * terms * height * height * width,
            bytes_accessed=4 * terms * height * width,
            transcendentals=0,
        ),
    )(partner, sector_sizes, wavefunction, diagonal, left_ops, right_ops)

    energy = energy[0, 0]
    row_index = lax.axis_index("op") * rows + jnp.arange(rows, dtype=jnp.int32)
    col_index = jnp.arange(width, dtype=jnp.int32)
    live_mask = (row_index[None, :, None] < sector_sizes[:, None, None]) & (
        col_index[None, None, :] < sector_sizes[:, None, None]
    )
    wave = jnp.where(live_mask, wavefunction, jnp.zeros_like(wavefunction)).astype(F32)
    residual = sigma - energy * wave
    updated = wave - residual / jnp.maximum(jnp.abs(diagonal - energy), 1.0)
    return (updated, residual)


def solution(mesh):
    return jax.shard_map(
        functools.partial(per_device, mesh.shape["sec"], mesh.shape["op"]),
        mesh=mesh,
        in_specs=(
            P("sec", "op", None),
            P("sec", "op", None, None),
            P("sec", "op", None, None),
            P("sec", "op", None),
            P("sec"),
            P(),
        ),
        out_specs=(P("sec", "op", None), P("sec", "op", None)),
        check_vma=False,
    )
```

profile of v0, /device:TPU:0, one launch (start us, length us, event | category | flops | bytes accessed | tf_op | source)
XLA Modules:
  0.0 67.5 jit_solution(7228895753813477024)
XLA Ops:
  1.3 0.0 copy-start
  1.3 0.0 copy-start.1
  1.3 63.7 %shard_map.77 = (f32[1,96,768]{2,1,0:T(8,128)}, f32[1,1]{1,0:T(1,128)}) custom-call(s32[4]{0:T(128)} %partner_ref.1, s32[1]{0:T(128)} %copy.8.sizes_ref, bf16[1,96,768]{2,1,0:T(8,128)(2,1)} %wave_ref.1, f32[1,96,768]{2,1,0:T(8,128)} %diag_ref.1, bf16[1,3,768,768]{3,2,1,0:T(8,128)(2,1)} %left_hbm.1, bf16[1,3,768,768]{3,2,1,0:T(8,128)(2,1)} %right_hbm.1), custom_call_target="tpu_custom_call" | custom-call | flops 10871635968 | bytes 7077888 | tf_op jit(solution)/shard_map/pallas_call | solution.py:340
  65.0 0.0 copy-done
  65.0 0.0 copy-done.1
  65.0 2.5 %convert_subtract_fusion = (f32[1,96,768]{2,1,0:T(8,128)}, f32[1,96,768]{2,1,0:T(8,128)}) fusion(f32[1,96,768]{2,1,0:T(8,128)S(1)} %copy-done, f32[]{:T(128)} %bitcast.1, bf16[1,96,768]{2,1,0:T(8,128)(2,1)S(1)} %copy-done.1, pred[768]{0:T(1024)(128)(4,1)S(1)} %iota_compare_fusion, pred[96]{0:T(512)(128)(4,1)S(1)} %add_compare_fusion, ...), kind=kLoop, calls=%fused_computation | loop fusion | flops 737280 | bytes 1327972 | tf_op jit(solution)/shard_map/sub | solution.py:386
  (2 shorter events, 0.0 us)
Async XLA Ops:
  1.3 63.7 %copy-start = (f32[1,96,768]{2,1,0:T(8,128)S(1)}, f32[1,96,768]{2,1,0:T(8,128)}, u32[]{:S(2)}) copy-start(f32[1,96,768]{2,1,0:T(8,128)} %diag_ref.1) | copy-start | bytes 884740
  1.3 63.7 %copy-start.1 = (bf16[1,96,768]{2,1,0:T(8,128)(2,1)S(1)}, bf16[1,96,768]{2,1,0:T(8,128)(2,1)}, u32[]{:S(2)}) copy-start(bf16[1,96,768]{2,1,0:T(8,128)(2,1)} %wave_ref.1) | copy-start | bytes 442372
where the time goes:
time: 67.7 us; the launch traced here: 67.5 us
  Pallas kernels  63.7 us (94%)
  other arithmetic  2.49 us (4%)
  between operations  1.33 us (2%)
    pallas_call x1, Pallas kernels, per_device(): pl.pallas_call(functools.partial(kernel, sectors, ops), out_shape=(jax.Sh...  63.7 us
    sub x1, other arithmetic, per_device(): updated = wave - residual / jnp.maximum(jnp.abs(diagonal - energy), 1.0)  2.48 us

commit v1 on v0

--- a/solution.py
+++ b/solution.py
@@ -40,7 +40,7 @@
     scalars, scalar_y, scalar_z, scalar_s,
     load_sem,
     chain_send, chain_recv, near_send, near_recv,
-    sec_send, sec_recv, mate_send, mate_recv, route_send, route_recv,
+    sec_send, sec_recv, swap_send, swap_recv, mate_send, mate_recv, route_send, route_recv,
     adj_send, adj_recv, dir_send, dir_recv, sc_send, sc_recv,
 ):
     far_count = ops // PAIR
@@ -124,7 +124,7 @@
     def to_chips(cond, half, place):
         block = blocks.at[me_sec, half, place]
         for step in range(1, sec_far):
-            args = (block, block, sec_send.at[step, half, place], sec_recv.at[step, half], chip_peer(step))
+            args = (block, block, sec_send.at[step, half, place], sec_recv.at[step, half, place], chip_peer(step))
             send(*args) if cond is None else send_if(cond, *args)
 
     mine = blocks.at[me_sec, near, far]
@@ -164,9 +164,21 @@
         part = blocks.at[sector, half]
         send(part, part, mate_send.at[step, half], mate_recv.at[step, half], mate)
 
+    beside = far + 1 - 2 * lax.rem(far, PAIR)
+    rest = []
+    for step in range(1, far_count // PAIR):
+        base = lax.rem(far // PAIR + step, far_count // PAIR) * PAIR
+        rest += [base, base + 1]
+    for place in (far, beside):
+        for step in range(1, sec_far):
+            block = blocks.at[chip_at(-step) + core, near, place]
+            recv(block, sec_send.at[step, near, place], sec_recv.at[step, near, place])
+            send(block, block, swap_send.at[step, place], swap_recv.at[step, place], near_peer)
+
     to_mate(me_sec, 0, near)
-    for step in range(far_count):
-        place = far_at(-step)
+    for place in (far, beside):
+        recv(blocks.at[me_sec, 1 - near, place], near_send.at[place], near_recv.at[place])
+    for place in rest:
         recv(blocks.at[me_sec, 1 - near, place], near_send.at[place], near_recv.at[place])
         to_chips(None, 1 - near, place)
     to_mate(me_sec, 0, 1 - near)
@@ -239,10 +251,14 @@
             total = total + zr[step].astype(F32)
         return total
 
-    def from_chips(half):
+    def from_chips(half, direct_half):
         for step in range(1, sec_far):
             sector = chip_at(-step) + core
-            recv(blocks.at[sector, half], sec_send.at[step, half, 0], sec_recv.at[step, half])
+            if not direct_half:
+                for place in (far, beside):
+                    recv(blocks.at[sector, half, place], swap_send.at[step, place], swap_recv.at[step, place])
+            for place in rest:
+                recv(blocks.at[sector, half, place], sec_send.at[step, half, place], sec_recv.at[step, half, place])
             to_mate(sector, step, half)
 
     adj = (adj_keep, adj_ys, adj_yr, adj_send, adj_recv)
@@ -252,11 +268,11 @@
     second_base = len(groups[0]) * span
 
     products(groups[0], 0, left_t, own_full, nn_dot, *adj)
-    from_chips(near)
+    from_chips(near, True)
     products(groups[1], second_base, left_t, own_full, nn_dot, *adj)
     for step in groups[0]:
         pass_on(step, *adj_pass)
-    from_chips(1 - near)
+    from_chips(1 - near, False)
     for step in range(sec_far):
         sector = chip_at(-step) + (1 - core)
         for side in (near, 1 - near):
@@ -359,7 +375,8 @@
             pltpu.VMEM((sectors, 2, 8, 128), F32),
             dma((2,)),
             dma((2, far_count)), *[dma((far_count,))] * 3,
-            dma((sec_far, PAIR, far_count)), dma((sec_far, PAIR)),
+            *[dma((sec_far, PAIR, far_count))] * 2,
+            *[dma((sec_far, far_count))] * 2,
             *[dma((sec_far, PAIR))] * 2,
             *[dma((2, sec_far))] * 2,
             *[dma((2 * far_count,))] * 4,

time: 67.7 us -> 69.3 us (1.024)
  Pallas kernels: 63.7 us -> 65.3 us
    pallas_call x1, Pallas kernels: 63.7 us -> 65.3 us  [per_device(): pl.pallas_call(functools.partial(kernel, sectors, ops), out_shape=(jax.Sh...]
where the time goes in v1:
time: 69.3 us; the launch traced here: 69.1 us
  Pallas kernels  65.3 us (94%)
  other arithmetic  2.49 us (4%)
  between operations  1.33 us (2%)
    pallas_call x1, Pallas kernels, per_device(): pl.pallas_call(functools.partial(kernel, sectors, ops), out_shape=(jax.Sh...  65.3 us
    sub x1, other arithmetic, per_device(): updated = wave - residual / jnp.maximum(jnp.abs(diagonal - energy), 1.0)  2.48 us

profile of v1, /device:TPU:0, one launch (start us, length us, event | category | flops | bytes accessed | tf_op | source)
XLA Modules:
  0.0 69.1 jit_solution(15674843127237140072)
XLA Ops:
  1.3 0.0 copy-start
  1.3 0.0 copy-start.1
  1.3 65.3 %shard_map.77 = (f32[1,96,768]{2,1,0:T(8,128)}, f32[1,1]{1,0:T(1,128)}) custom-call(s32[4]{0:T(128)} %partner_ref.1, s32[1]{0:T(128)} %copy.8.sizes_ref, bf16[1,96,768]{2,1,0:T(8,128)(2,1)} %wave_ref.1, f32[1,96,768]{2,1,0:T(8,128)} %diag_ref.1, bf16[1,3,768,768]{3,2,1,0:T(8,128)(2,1)} %left_hbm.1, bf16[1,3,768,768]{3,2,1,0:T(8,128)(2,1)} %right_hbm.1), custom_call_target="tpu_custom_call" | custom-call | flops 10871635968 | bytes 7077888 | tf_op jit(solution)/shard_map/pallas_call | solution.py:356
  66.6 0.0 copy-done
  66.6 0.0 copy-done.1
  66.6 2.5 %convert_subtract_fusion = (f32[1,96,768]{2,1,0:T(8,128)}, f32[1,96,768]{2,1,0:T(8,128)}) fusion(f32[1,96,768]{2,1,0:T(8,128)S(1)} %copy-done, f32[]{:T(128)} %bitcast.1, bf16[1,96,768]{2,1,0:T(8,128)(2,1)S(1)} %copy-done.1, pred[768]{0:T(1024)(128)(4,1)S(1)} %iota_compare_fusion, pred[96]{0:T(512)(128)(4,1)S(1)} %add_compare_fusion, ...), kind=kLoop, calls=%fused_computation | loop fusion | flops 737280 | bytes 1327972 | tf_op jit(solution)/shard_map/sub | solution.py:403
  (2 shorter events, 0.0 us)
Async XLA Ops:
  1.3 65.3 %copy-start = (f32[1,96,768]{2,1,0:T(8,128)S(1)}, f32[1,96,768]{2,1,0:T(8,128)}, u32[]{:S(2)}) copy-start(f32[1,96,768]{2,1,0:T(8,128)} %diag_ref.1) | copy-start | bytes 884740
  1.3 65.3 %copy-start.1 = (bf16[1,96,768]{2,1,0:T(8,128)(2,1)S(1)}, bf16[1,96,768]{2,1,0:T(8,128)(2,1)}, u32[]{:S(2)}) copy-start(bf16[1,96,768]{2,1,0:T(8,128)(2,1)} %wave_ref.1) | copy-start | bytes 442372

commit v2 on v0

--- a/solution.py
+++ b/solution.py
@@ -34,7 +34,7 @@
     sectors, ops,
     partner_ref, sizes_ref, wave_ref, diag_ref, left_hbm, right_hbm,
     sigma_ref, energy_ref,
-    left, right, left_t, blocks, own_full, other_full, acc,
+    left, right, left_t, blocks, own_full, other_full, inner, acc,
     adj_keep, adj_ys, adj_yr, adj_zs, adj_zr, routed,
     dir_keep, dir_ys, dir_yr, dir_zs, dir_zr,
     scalars, scalar_y, scalar_z, scalar_s,
@@ -189,25 +189,26 @@
     def place_of(step):
         return pl.ds(pl.multiple_of(far_at(step) * span, span), span)
 
-    def products(group, base, left_side, middle, last_dot, keep, ys, yr, sends, recvs):
-        total = acc.at[pl.ds(base, len(group) * span)]
-
+    def first_products(left_side, middle):
         def one(term, carry):
-            lhs = jnp.concatenate([left_side[term, place_of(step), :] for step in group], axis=0)
-            inner = nn_dot(lhs, middle[...]).astype(BF16)
-            out = last_dot(inner, right[term])
-
-            @pl.when(term == 0)
-            def _():
-                total[...] = out
-
-            @pl.when(term > 0)
-            def _():
-                total[...] += out
-
+            columns = pl.ds(pl.multiple_of(term * width, width), width)
+            inner[:, columns] = nn_dot(left_side[term], middle[...]).astype(BF16)
             return carry
 
         lax.fori_loop(0, terms, one, 0)
+
+    def adjoint_sum(lhs):
+        return nn_dot(lhs, right[...].reshape(terms * width, width))
+
+    def direct_sum(lhs):
+        total = nt_dot(lhs[:, :width], right[0])
+        for term in range(1, terms):
+            total = total + nt_dot(lhs[:, term * width : (term + 1) * width], right[term])
+        return total
+
+    def products(group, base, term_sum, keep, ys, yr, sends, recvs):
+        lhs = jnp.concatenate([inner[place_of(step), :] for step in group], axis=0)
+        acc[base : base + len(group) * span, :] = term_sum(lhs)
         for at, step in enumerate(group):
             start = base + at * span
             first = acc[start : start + rows, :]
@@ -251,9 +252,10 @@
     dir_pass = (dir_keep, dir_yr, dir_zs, dir_zr, dir_send, dir_recv)
     second_base = len(groups[0]) * span
 
-    products(groups[0], 0, left_t, own_full, nn_dot, *adj)
+    first_products(left_t, own_full)
+    products(groups[0], 0, adjoint_sum, *adj)
     from_chips(near)
-    products(groups[1], second_base, left_t, own_full, nn_dot, *adj)
+    products(groups[1], second_base, adjoint_sum, *adj)
     for step in groups[0]:
         pass_on(step, *adj_pass)
     from_chips(1 - near)
@@ -265,10 +267,11 @@
     inner_product(groups[0], 0, other_full)
     inner_product(groups[1], second_base, other_full)
 
-    products(groups[0], 0, left, other_full, nt_dot, *direct)
+    first_products(left, other_full)
+    products(groups[0], 0, direct_sum, *direct)
     for step in groups[1]:
         pass_on(step, *adj_pass)
-    products(groups[1], second_base, left, other_full, nt_dot, *direct)
+    products(groups[1], second_base, direct_sum, *direct)
     for step in groups[0]:
         pass_on(step, *dir_pass)
     inner_product(groups[0], 0, own_full)
@@ -349,6 +352,7 @@
             operators, operators, operators,
             pltpu.VMEM((sectors, PAIR, far_count, rows, width), BF16),
             full, full,
+            pltpu.VMEM((height, terms * width), BF16),
             pltpu.VMEM((height, width), F32),
             block32, block16, block16, block16, block16,
             pltpu.VMEM((sectors, rows, width), F32),

time: 67.7 us -> 70.8 us (1.046)
  Pallas kernels: 63.7 us -> 66.8 us
    pallas_call x1, Pallas kernels: 63.7 us -> 66.8 us  [per_device(): pl.pallas_call(functools.partial(kernel, sectors, ops), out_shape=(jax.Sh...]
where the time goes in v2:
time: 70.8 us; the launch traced here: 70.6 us
  Pallas kernels  66.8 us (94%)
  other arithmetic  2.49 us (4%)
  between operations  1.33 us (2%)
    pallas_call x1, Pallas kernels, per_device(): pl.pallas_call(functools.partial(kernel, sectors, ops), out_shape=(jax.Sh...  66.8 us
    sub x1, other arithmetic, per_device(): updated = wave - residual / jnp.maximum(jnp.abs(diagonal - energy), 1.0)  2.48 us

profile of v2, /device:TPU:0, one launch (start us, length us, event | category | flops | bytes accessed | tf_op | source)
XLA Modules:
  0.0 70.6 jit_solution(7365211587524699066)
XLA Ops:
  1.3 0.0 copy-start
  1.3 0.0 copy-start.1
  1.3 66.8 %shard_map.77 = (f32[1,96,768]{2,1,0:T(8,128)}, f32[1,1]{1,0:T(1,128)}) custom-call(s32[4]{0:T(128)} %partner_ref.1, s32[1]{0:T(128)} %copy.8.sizes_ref, bf16[1,96,768]{2,1,0:T(8,128)(2,1)} %wave_ref.1, f32[1,96,768]{2,1,0:T(8,128)} %diag_ref.1, bf16[1,3,768,768]{3,2,1,0:T(8,128)(2,1)} %left_hbm.1, bf16[1,3,768,768]{3,2,1,0:T(8,128)(2,1)} %right_hbm.1), custom_call_target="tpu_custom_call" | custom-call | flops 10871635968 | bytes 7077888 | tf_op jit(solution)/shard_map/pallas_call | solution.py:343
  68.1 0.0 copy-done
  68.1 0.0 copy-done.1
  68.1 2.5 %convert_subtract_fusion = (f32[1,96,768]{2,1,0:T(8,128)}, f32[1,96,768]{2,1,0:T(8,128)}) fusion(f32[1,96,768]{2,1,0:T(8,128)S(1)} %copy-done, f32[]{:T(128)} %bitcast.1, bf16[1,96,768]{2,1,0:T(8,128)(2,1)S(1)} %copy-done.1, pred[768]{0:T(1024)(128)(4,1)S(1)} %iota_compare_fusion, pred[96]{0:T(512)(128)(4,1)S(1)} %add_compare_fusion, ...), kind=kLoop, calls=%fused_computation | loop fusion | flops 737280 | bytes 1327972 | tf_op jit(solution)/shard_map/sub | solution.py:390
  (2 shorter events, 0.0 us)
Async XLA Ops:
  1.3 66.8 %copy-start = (f32[1,96,768]{2,1,0:T(8,128)S(1)}, f32[1,96,768]{2,1,0:T(8,128)}, u32[]{:S(2)}) copy-start(f32[1,96,768]{2,1,0:T(8,128)} %diag_ref.1) | copy-start | bytes 884740
  1.3 66.8 %copy-start.1 = (bf16[1,96,768]{2,1,0:T(8,128)(2,1)S(1)}, bf16[1,96,768]{2,1,0:T(8,128)(2,1)}, u32[]{:S(2)}) copy-start(bf16[1,96,768]{2,1,0:T(8,128)(2,1)} %wave_ref.1) | copy-start | bytes 442372

commit v3 on v0

--- a/solution.py
+++ b/solution.py
@@ -34,7 +34,7 @@
     sectors, ops,
     partner_ref, sizes_ref, wave_ref, diag_ref, left_hbm, right_hbm,
     sigma_ref, energy_ref,
-    left, right, left_t, blocks, own_full, other_full, acc,
+    left, right, left_t, blocks, own_full, other_full, lhs, inner, acc,
     adj_keep, adj_ys, adj_yr, adj_zs, adj_zr, routed,
     dir_keep, dir_ys, dir_yr, dir_zs, dir_zr,
     scalars, scalar_y, scalar_z, scalar_s,
@@ -189,25 +189,38 @@
     def place_of(step):
         return pl.ds(pl.multiple_of(far_at(step) * span, span), span)
 
-    def products(group, base, left_side, middle, last_dot, keep, ys, yr, sends, recvs):
-        total = acc.at[pl.ds(base, len(group) * span)]
+    tile = 256 if width % 256 == 0 else width
+
+    def tile_at(index):
+        return pl.ds(pl.multiple_of(index * tile, tile), tile)
+
+    def adjoint_tile(part, term, columns):
+        return nn_dot(part, right[term, :, columns])
+
+    def direct_tile(part, term, columns):
+        return nt_dot(part, right[term, columns, :])
+
+    def products(group, base, left_side, middle, last_tile, keep, ys, yr, sends, recvs):
+        count = len(group) * span
 
         def one(term, carry):
-            lhs = jnp.concatenate([left_side[term, place_of(step), :] for step in group], axis=0)
-            inner = nn_dot(lhs, middle[...]).astype(BF16)
-            out = last_dot(inner, right[term])
-
-            @pl.when(term == 0)
-            def _():
-                total[...] = out
-
-            @pl.when(term > 0)
-            def _():
-                total[...] += out
-
+            for at, step in enumerate(group):
+                lhs[at * span : (at + 1) * span, :] = left_side[term, place_of(step), :]
+            for index in range(width // tile):
+                columns = slice(index * tile, (index + 1) * tile)
+                inner[term, :count, columns] = nn_dot(lhs[:count, :], middle[:, columns]).astype(BF16)
             return carry
 
+        def two(index, carry):
+            columns = tile_at(index)
+            total = last_tile(inner[0, :count, :], 0, columns)
+            for term in range(1, terms):
+                total = total + last_tile(inner[term, :count, :], term, columns)
+            acc[base : base + count, columns] = total
+            return carry
+
         lax.fori_loop(0, terms, one, 0)
+        lax.fori_loop(0, width // tile, two, 0)
         for at, step in enumerate(group):
             start = base + at * span
             first = acc[start : start + rows, :]
@@ -251,9 +264,9 @@
     dir_pass = (dir_keep, dir_yr, dir_zs, dir_zr, dir_send, dir_recv)
     second_base = len(groups[0]) * span
 
-    products(groups[0], 0, left_t, own_full, nn_dot, *adj)
+    products(groups[0], 0, left_t, own_full, adjoint_tile, *adj)
     from_chips(near)
-    products(groups[1], second_base, left_t, own_full, nn_dot, *adj)
+    products(groups[1], second_base, left_t, own_full, adjoint_tile, *adj)
     for step in groups[0]:
         pass_on(step, *adj_pass)
     from_chips(1 - near)
@@ -265,10 +278,10 @@
     inner_product(groups[0], 0, other_full)
     inner_product(groups[1], second_base, other_full)
 
-    products(groups[0], 0, left, other_full, nt_dot, *direct)
+    products(groups[0], 0, left, other_full, direct_tile, *direct)
     for step in groups[1]:
         pass_on(step, *adj_pass)
-    products(groups[1], second_base, left, other_full, nt_dot, *direct)
+    products(groups[1], second_base, left, other_full, direct_tile, *direct)
     for step in groups[0]:
         pass_on(step, *dir_pass)
     inner_product(groups[0], 0, own_full)
@@ -348,7 +361,7 @@
         scratch_shapes=[
             operators, operators, operators,
             pltpu.VMEM((sectors, PAIR, far_count, rows, width), BF16),
-            full, full,
+            full, full, full, operators,
             pltpu.VMEM((height, width), F32),
             block32, block16, block16, block16, block16,
             pltpu.VMEM((sectors, rows, width), F32),

time: 67.7 us -> 67.6 us (level)
  no operation moved by 1% of the time
where the time goes in v3:
time: 67.6 us; the launch traced here: 67.4 us
  Pallas kernels  63.6 us (94%)
  other arithmetic  2.49 us (4%)
  between operations  1.33 us (2%)
    pallas_call x1, Pallas kernels, per_device(): pl.pallas_call(functools.partial(kernel, sectors, ops), out_shape=(jax.Sh...  63.6 us
    sub x1, other arithmetic, per_device(): updated = wave - residual / jnp.maximum(jnp.abs(diagonal - energy), 1.0)  2.48 us

profile of v3, /device:TPU:0, one launch (start us, length us, event | category | flops | bytes accessed | tf_op | source)
XLA Modules:
  0.0 67.4 jit_solution(15851127769908823527)
XLA Ops:
  1.3 0.0 copy-start
  1.3 0.0 copy-start.1
  1.3 63.6 %shard_map.77 = (f32[1,96,768]{2,1,0:T(8,128)}, f32[1,1]{1,0:T(1,128)}) custom-call(s32[4]{0:T(128)} %partner_ref.1, s32[1]{0:T(128)} %copy.8.sizes_ref, bf16[1,96,768]{2,1,0:T(8,128)(2,1)} %wave_ref.1, f32[1,96,768]{2,1,0:T(8,128)} %diag_ref.1, bf16[1,3,768,768]{3,2,1,0:T(8,128)(2,1)} %left_hbm.1, bf16[1,3,768,768]{3,2,1,0:T(8,128)(2,1)} %right_hbm.1), custom_call_target="tpu_custom_call" | custom-call | flops 10871635968 | bytes 7077888 | tf_op jit(solution)/shard_map/pallas_call | solution.py:353
  64.9 0.0 copy-done
  65.0 0.0 copy-done.1
  65.0 2.5 %convert_subtract_fusion = (f32[1,96,768]{2,1,0:T(8,128)}, f32[1,96,768]{2,1,0:T(8,128)}) fusion(f32[1,96,768]{2,1,0:T(8,128)S(1)} %copy-done, f32[]{:T(128)} %bitcast.1, bf16[1,96,768]{2,1,0:T(8,128)(2,1)S(1)} %copy-done.1, pred[768]{0:T(1024)(128)(4,1)S(1)} %iota_compare_fusion, pred[96]{0:T(512)(128)(4,1)S(1)} %add_compare_fusion, ...), kind=kLoop, calls=%fused_computation | loop fusion | flops 737280 | bytes 1327972 | tf_op jit(solution)/shard_map/sub | solution.py:399
  (2 shorter events, 0.0 us)
Async XLA Ops:
  1.3 63.6 %copy-start = (f32[1,96,768]{2,1,0:T(8,128)S(1)}, f32[1,96,768]{2,1,0:T(8,128)}, u32[]{:S(2)}) copy-start(f32[1,96,768]{2,1,0:T(8,128)} %diag_ref.1) | copy-start | bytes 884740
  1.3 63.6 %copy-start.1 = (bf16[1,96,768]{2,1,0:T(8,128)(2,1)S(1)}, bf16[1,96,768]{2,1,0:T(8,128)(2,1)}, u32[]{:S(2)}) copy-start(bf16[1,96,768]{2,1,0:T(8,128)(2,1)} %wave_ref.1) | copy-start | bytes 442372

commit v4 on v3

--- a/solution.py
+++ b/solution.py
@@ -34,7 +34,7 @@
     sectors, ops,
     partner_ref, sizes_ref, wave_ref, diag_ref, left_hbm, right_hbm,
     sigma_ref, energy_ref,
-    left, right, left_t, blocks, own_full, other_full, lhs, inner, acc,
+    left, right, left_t, blocks, own_full, other_full, lhs, inner, adj_acc, dir_acc,
     adj_keep, adj_ys, adj_yr, adj_zs, adj_zr, routed,
     dir_keep, dir_ys, dir_yr, dir_zs, dir_zr,
     scalars, scalar_y, scalar_z, scalar_s,
@@ -183,8 +183,9 @@
     load_right.wait()
 
     order = list(range(1, far_count)) + [0]
-    half = (far_count + 1) // 2
-    groups = [order[:half], order[half:]]
+    quarter = max(far_count // 4, 1)
+    groups = [order[:quarter], order[quarter:-quarter], order[-quarter:]]
+    bases = [0, quarter * span, (far_count - quarter) * span]
 
     def place_of(step):
         return pl.ds(pl.multiple_of(far_at(step) * span, span), span)
@@ -200,7 +201,8 @@
     def direct_tile(part, term, columns):
         return nt_dot(part, right[term, columns, :])
 
-    def products(group, base, left_side, middle, last_tile, keep, ys, yr, sends, recvs):
+    def products(which, left_side, middle, last_tile, acc, keep, ys, yr, sends, recvs):
+        group, base = groups[which], bases[which]
         count = len(group) * span
 
         def one(term, carry):
@@ -229,9 +231,9 @@
             ys[step] = jnp.where(near == 0, second, first).astype(BF16)
             send(ys.at[step], yr.at[step], sends.at[step], recvs.at[step], near_peer)
 
-    def inner_product(group, base, weight):
-        for at, step in enumerate(group):
-            start = base + at * span
+    def inner_product(which, acc, weight):
+        for at, step in enumerate(groups[which]):
+            start = bases[which] + at * span
             scalars[0] += fold_sum(acc[start : start + span, :] * weight[place_of(step), :].astype(F32))
 
     def pass_on(step, keep, yr, zs, zr, sends, recvs):
@@ -258,34 +260,36 @@
             recv(blocks.at[sector, half], sec_send.at[step, half, 0], sec_recv.at[step, half])
             to_mate(sector, step, half)
 
-    adj = (adj_keep, adj_ys, adj_yr, adj_send, adj_recv)
-    direct = (dir_keep, dir_ys, dir_yr, dir_send, dir_recv)
+    adj = (adj_acc, adj_keep, adj_ys, adj_yr, adj_send, adj_recv)
+    direct = (dir_acc, dir_keep, dir_ys, dir_yr, dir_send, dir_recv)
     adj_pass = (adj_keep, adj_yr, adj_zs, adj_zr, adj_send, adj_recv)
     dir_pass = (dir_keep, dir_yr, dir_zs, dir_zr, dir_send, dir_recv)
-    second_base = len(groups[0]) * span
-
-    products(groups[0], 0, left_t, own_full, adjoint_tile, *adj)
+
+    products(0, left_t, own_full, adjoint_tile, *adj)
     from_chips(near)
-    products(groups[1], second_base, left_t, own_full, adjoint_tile, *adj)
+    products(1, left_t, own_full, adjoint_tile, *adj)
     for step in groups[0]:
         pass_on(step, *adj_pass)
+    products(2, left_t, own_full, adjoint_tile, *adj)
     from_chips(1 - near)
+    for step in groups[1]:
+        pass_on(step, *adj_pass)
     for step in range(sec_far):
         sector = chip_at(-step) + (1 - core)
         for side in (near, 1 - near):
             recv(blocks.at[sector, side], mate_send.at[step, side], mate_recv.at[step, side])
     assemble(partner_ref[me_sec], other_full)
-    inner_product(groups[0], 0, other_full)
-    inner_product(groups[1], second_base, other_full)
-
-    products(groups[0], 0, left, other_full, direct_tile, *direct)
-    for step in groups[1]:
+
+    products(0, left, other_full, direct_tile, *direct)
+    for step in groups[2]:
         pass_on(step, *adj_pass)
-    products(groups[1], second_base, left, other_full, direct_tile, *direct)
+    products(1, left, other_full, direct_tile, *direct)
     for step in groups[0]:
         pass_on(step, *dir_pass)
-    inner_product(groups[0], 0, own_full)
-    inner_product(groups[1], second_base, own_full)
+    products(2, left, other_full, direct_tile, *direct)
+    for which in range(3):
+        inner_product(which, adj_acc, other_full)
+        inner_product(which, dir_acc, own_full)
 
     send(scalars, scalar_y, sc_send.at[0], sc_recv.at[0], near_peer)
     routed[me_sec] = finish(adj_keep, adj_zr, adj_send, adj_recv)
@@ -297,7 +301,7 @@
     scalar_z[0] = scalars[...] + scalar_y[...]
     for step in range(1, far_count):
         send(scalar_z.at[0], scalar_z.at[step], sc_send.at[step], sc_recv.at[step], far_peer(step))
-    for step in groups[1]:
+    for step in groups[1] + groups[2]:
         pass_on(step, *dir_pass)
 
     inner_sum = scalar_z[0]
@@ -362,7 +366,7 @@
             operators, operators, operators,
             pltpu.VMEM((sectors, PAIR, far_count, rows, width), BF16),
             full, full, full, operators,
-            pltpu.VMEM((height, width), F32),
+            *[pltpu.VMEM((height, width), F32)] * 2,
             block32, block16, block16, block16, block16,
             pltpu.VMEM((sectors, rows, width), F32),
             block32, block16, block16, block16, block16,

time: 67.6 us -> 70.5 us (1.043)
  Pallas kernels: 63.6 us -> 66.2 us
    pallas_call x1, Pallas kernels: 63.6 us -> 66.2 us  [per_device(): pl.pallas_call(functools.partial(kernel, sectors, ops), out_shape=(jax.Sh...]
where the time goes in v4:
time: 70.5 us; the launch traced here: 70 us
  Pallas kernels  66.2 us (94%)
  other arithmetic  2.49 us (4%)
  between operations  1.33 us (2%)
    pallas_call x1, Pallas kernels, per_device(): pl.pallas_call(functools.partial(kernel, sectors, ops), out_shape=(jax.Sh...  66.2 us
    sub x1, other arithmetic, per_device(): updated = wave - residual / jnp.maximum(jnp.abs(diagonal - energy), 1.0)  2.48 us

profile of v4, /device:TPU:0, one launch (start us, length us, event | category | flops | bytes accessed | tf_op | source)
XLA Modules:
  0.0 70.0 jit_solution(1078171988191282120)
XLA Ops:
  1.3 0.0 copy-start
  1.3 0.0 copy-start.1
  1.3 66.2 %shard_map.77 = (f32[1,96,768]{2,1,0:T(8,128)}, f32[1,1]{1,0:T(1,128)}) custom-call(s32[4]{0:T(128)} %partner_ref.1, s32[1]{0:T(128)} %copy.8.sizes_ref, bf16[1,96,768]{2,1,0:T(8,128)(2,1)} %wave_ref.1, f32[1,96,768]{2,1,0:T(8,128)} %diag_ref.1, bf16[1,3,768,768]{3,2,1,0:T(8,128)(2,1)} %left_hbm.1, bf16[1,3,768,768]{3,2,1,0:T(8,128)(2,1)} %right_hbm.1), custom_call_target="tpu_custom_call" | custom-call | flops 10871635968 | bytes 7077888 | tf_op jit(solution)/shard_map/pallas_call | solution.py:357
  67.5 0.0 copy-done
  67.5 0.0 copy-done.1
  67.5 2.5 %convert_subtract_fusion = (f32[1,96,768]{2,1,0:T(8,128)}, f32[1,96,768]{2,1,0:T(8,128)}) fusion(f32[1,96,768]{2,1,0:T(8,128)S(1)} %copy-done, f32[]{:T(128)} %bitcast.1, bf16[1,96,768]{2,1,0:T(8,128)(2,1)S(1)} %copy-done.1, pred[768]{0:T(1024)(128)(4,1)S(1)} %iota_compare_fusion, pred[96]{0:T(512)(128)(4,1)S(1)} %add_compare_fusion, ...), kind=kLoop, calls=%fused_computation | loop fusion | flops 737280 | bytes 1327972 | tf_op jit(solution)/shard_map/sub | solution.py:403
  (2 shorter events, 0.0 us)
Async XLA Ops:
  1.3 66.2 %copy-start = (f32[1,96,768]{2,1,0:T(8,128)S(1)}, f32[1,96,768]{2,1,0:T(8,128)}, u32[]{:S(2)}) copy-start(f32[1,96,768]{2,1,0:T(8,128)} %diag_ref.1) | copy-start | bytes 884740
  1.3 66.2 %copy-start.1 = (bf16[1,96,768]{2,1,0:T(8,128)(2,1)S(1)}, bf16[1,96,768]{2,1,0:T(8,128)(2,1)}, u32[]{:S(2)}) copy-start(bf16[1,96,768]{2,1,0:T(8,128)(2,1)} %wave_ref.1) | copy-start | bytes 442372
